TPU v7x, 128 devices: a whole 4x4x4 slice. The times are simulated.
128 devices in a mesh: zonal: 16 (over z_lo, y, core), merid: 8 (over x, z_hi).
Axes of the slice: x: 4, y: 4, z: 4 (z_hi: 2, z_lo: 2; z = z_hi * 2 + z_lo), core: 2. Of those that a mesh axis runs over, the one named last changes fastest.
Arguments:
- field: bfloat16 [200, 128, 2048], P(None, 'merid', 'zonal'), may hold values from -6 to 6
- land_mask: int32 [128, 2048], P('merid', 'zonal'), may hold values 0 or 1
- fold_partner: int32 [2048], replicated, may hold values from 0 to 2047, as said below
- dw_kernel: bfloat16 [3, 200, 7, 7], replicated, may hold values from -0.875 to 0.875
- norm_gain: bfloat16 [3, 200], replicated, may hold values from 0.25 to 1.75
- w_in: bfloat16 [3, 200, 800], replicated, may hold values from -0.4375 to 0.4375
- w_out: bfloat16 [3, 800, 200], replicated, may hold values from -0.21875 to 0.21875
Outputs:
- state: bfloat16 [200, 128, 2048], P(None, 'merid', 'zonal')
Inputs may be any that keep to these rules, and one draw needn't show every extreme that they name: fold_partner[j] = (s - j) mod 2048 for one s.
All inputs are finite; a program needn't handle non-finite values. No bound on the sum of `land_mask` on one device may be relied on, other than what follows from the above.
Results may differ from a plain program's by a relative error of at most 0.012.
Values may be sent and summed in bfloat16 or wider, within the bound.
No kernel may reach another device: no remote copies, remote signals or barrier semaphores. Data moves between devices by JAX's collectives and lax.ppermute only.
A program may use at most 128 MiB of HBM per device.

v0:
```python
import jax
import jax.numpy as jnp
import numpy as np
from jax import lax
from jax.experimental import pallas as pl
from jax.experimental.pallas import tpu as pltpu
from jax.sharding import PartitionSpec as P

BLOCKS = 3
C = 200
PAD = 208
H = 800
ROWS = 16
LANES = 128
GROUPS = C // 8
MAIN = 8 * ROWS
SIDE = 8 * 6
EPS = 1e-05
F32 = jnp.float32
BF16 = jnp.bfloat16
EDGE_ROWS = (0, 1, 2, 13, 14, 15)
PACK = 40
SEND = PAD + 3 * C + 2 * PACK + 8
SWAP = 3 * C + PACK
BOT = 3 * C + 8
VM = pl.BlockSpec(memory_space=pltpu.VMEM)
SM = pl.BlockSpec(memory_space=pltpu.SMEM)


def dot32(a, b):
    return jnp.dot(a, b, preferred_element_type=F32)


def lanes_bf16(rows):
    return lax.broadcasted_iota(jnp.int32, (rows, LANES), 1).astype(F32).astype(BF16)


def pack_corner(v):
    lane = lax.broadcasted_iota(jnp.int32, (PACK, LANES), 1)
    packed = v[:PACK]
    for q in range(1, C // PACK):
        packed = jnp.where(lane >= 24 * q, pltpu.roll(v[PACK * q : PACK * (q + 1)], 24 * q, 1), packed)
    return packed


def band_kernel(block, taps_ref, w_in_ref, gain_ref, main_ref, side_ref, w1_ref, gains_ref):
    rows = [jnp.concatenate([taps_ref[block, a].astype(F32), jnp.zeros((1, C), F32)], axis=0) for a in range(7)]
    taps = jnp.concatenate(rows + [jnp.zeros((8, C), F32)], axis=0).T.astype(BF16)

    def place(first, second, tap_of, own, out_ref, at):
        depth = own.shape[1]
        tap = lax.broadcasted_iota(jnp.int32, (64, depth), 0)
        both = []
        for i in (first, second):
            spread = jnp.where(tap == tap_of(i), 1.0, 0.0).astype(BF16)
            both.append(dot32(taps, spread).reshape(GROUPS, 8, depth))
        both = jnp.concatenate(both, axis=1).astype(BF16)
        out_ref[:, pl.ds(at, 16), :] = both * own[None]

    lane = lax.broadcasted_iota(jnp.int32, (1, 7 * MAIN), 1)
    e, row = lane // MAIN, lane % ROWS

    def main_tap(i):
        a = row + 3 - i
        return jnp.where((a >= 0) & (a < 7), 8 * a + e, -1)

    wide = lax.broadcasted_iota(jnp.int32, (16, 7 * MAIN), 1)
    high = lax.broadcasted_iota(jnp.int32, (16, 7 * MAIN), 0)
    own_main = jnp.where((wide % MAIN) // ROWS == high % 8, 1.0, 0.0).astype(BF16)

    def main_pair(p, carry):
        place(2 * p, 2 * p + 1, main_tap, own_main, main_ref, pl.multiple_of(16 * p, 16))
        return carry

    lax.fori_loop(0, ROWS // 2, main_pair, 0)
    lane = lax.broadcasted_iota(jnp.int32, (1, 7 * SIDE), 1)
    e_side, slot = lane // SIDE, lane % SIDE
    k = slot // 8
    row_side = jnp.where(k < 3, k, k + ROWS)

    def side_tap(i):
        a = row_side - i
        return jnp.where((a >= 0) & (a < 7), 8 * a + e_side, -1)

    wide = lax.broadcasted_iota(jnp.int32, (16, 7 * SIDE), 1)
    high = lax.broadcasted_iota(jnp.int32, (16, 7 * SIDE), 0)
    own_side = jnp.where(wide % 8 == high % 8, 1.0, 0.0).astype(BF16)
    for p in range(3):
        place(EDGE_ROWS[2 * p], EDGE_ROWS[2 * p + 1], side_tap, own_side, side_ref, 16 * p)
    w1_ref[...] = w_in_ref[block].T
    gain = gain_ref[...].astype(F32)[block : block + 1]
    gains_ref[...] = jnp.broadcast_to(gain, (LANES, C)).T


def make_bands(block, taps, w_in, gain):
    return pl.pallas_call(
        lambda *refs: band_kernel(block, *refs),
        out_shape=(
            jax.ShapeDtypeStruct((GROUPS, MAIN, 7 * MAIN), BF16),
            jax.ShapeDtypeStruct((GROUPS, SIDE, 7 * SIDE), BF16),
            jax.ShapeDtypeStruct((H, C), BF16),
            jax.ShapeDtypeStruct((C, LANES), F32),
        ),
        in_specs=[VM] * 3,
        out_specs=(VM,) * 4,
        compiler_params=pltpu.CompilerParams(vmem_limit_bytes=20 * 2**20),
        cost_estimate=pl.CostEstimate(flops=2 * 16 * 256 * 256 * 1024, bytes_accessed=9_000_000, transcendentals=0),
    )(taps, w_in, gain)


def emit_edges(tile_of, o_ref, out_ref, send_ref, bot_ref):
    lane = lanes_bf16(ROWS)

    def some(first, count):
        v = tile_of(first, count)
        o_ref[pl.ds(first * ROWS, count * ROWS), :] = v.reshape(count * ROWS, LANES)
        v = v.astype(BF16)
        if out_ref is not None:
            out_ref[pl.ds(first, count)] = v
        packed = pltpu.roll(v[0], 3, 1)
        for c in range(1, count):
            packed = jnp.where(lane >= 8 * c, pltpu.roll(v[c], 8 * c + 3, 1), packed)
        return packed

    for q in range(12):
        send_ref[16 * q : 16 * q + 16, :] = some(16 * q, 16)
    send_ref[192:208, :] = some(192, 8)
    wide = lax.broadcasted_iota(jnp.int32, (C, LANES), 1)

    def edge(first):
        rows = [o_ref[pl.ds(first + k, C, stride=ROWS), :] for k in range(3)]
        corner = pltpu.roll(rows[0], 3, 1)
        for k in range(1, 3):
            corner = jnp.where(wide >= 8 * k, pltpu.roll(rows[k], 8 * k + 3, 1), corner)
        return rows, pack_corner(corner)

    fill = jnp.zeros((8, LANES), F32)
    low, low_corner = edge(0)
    bot_ref[...] = jnp.concatenate(low + [fill], axis=0).astype(BF16)
    high, high_corner = edge(ROWS - 3)
    send_ref[PAD:, :] = jnp.concatenate(high + [low_corner, high_corner, fill], axis=0).astype(BF16)


EDGE_SHAPES = (
    jax.ShapeDtypeStruct((SEND, LANES), BF16),
    jax.ShapeDtypeStruct((BOT, LANES), BF16),
)


def first_kernel(x_ref, send_ref, bot_ref, o_ref):
    emit_edges(lambda first, count: x_ref[pl.ds(first, count)].astype(F32), o_ref, None, send_ref, bot_ref)


def first_edges(x):
    return pl.pallas_call(
        first_kernel,
        out_shape=EDGE_SHAPES,
        in_specs=[VM],
        out_specs=(VM,) * 2,
        scratch_shapes=[pltpu.VMEM((C * ROWS, LANES), F32)],
        compiler_params=pltpu.CompilerParams(vmem_limit_bytes=10 * 2**20),
    )(x)


def place_on_mesh():
    level = lax.axis_index("merid")
    return level == lax.axis_size("merid") - 1, level % 2


def turn_kernel(fold_ref, west_ref, east_ref, send_ref, bot_ref, q1_ref, q2_ref, up_ref):
    at_top, odd = place_on_mesh()
    off = (fold_ref[0] + (LANES // 2 + 1)) % LANES - LANES // 2
    lane = lax.broadcasted_iota(jnp.int32, (PACK, LANES), 1)
    parts = [ref[PAD:, :] for ref in (west_ref, send_ref, east_ref)]
    wide = [part.astype(F32) for part in parts]

    def corner(at):
        return jnp.where((lane & 7) < 3, wide[0][at : at + PACK], wide[2][at : at + PACK])

    @pl.when(jnp.logical_not(at_top))
    def _():
        up = jnp.concatenate([wide[1][: 3 * C], corner(3 * C + PACK)], axis=0)
        up_ref[...] = up.astype(BF16)

    @pl.when(at_top)
    def _():
        src = lax.broadcasted_iota(jnp.int32, (LANES, LANES), 0)
        dst = lax.broadcasted_iota(jnp.int32, (LANES, LANES), 1)
        slot = dst & 7
        col = jnp.where(slot < 3, slot - 3, slot + 125)
        used = slot < 6
        turned = jnp.zeros((SEND - PAD, LANES), F32)
        turned_corner = jnp.zeros((C, LANES), F32)
        for n in range(3):
            local_col = src + 128 * (n - 1)
            pick = jnp.where(local_col + dst == off + 127, 1.0, 0.0).astype(BF16)
            turned += dot32(parts[n], pick)
            hit = jnp.where(used & (local_col + col == off + 127), 1.0, 0.0)
            for k in range(3):
                pick = jnp.where(dst // 8 == k, hit, 0.0).astype(BF16)
                turned_corner += dot32(wide[n][(2 - k) * C : (3 - k) * C].astype(BF16), pick)
        rows = [turned[(2 - k) * C : (3 - k) * C] for k in range(3)]
        up_ref[...] = jnp.concatenate(rows + [pack_corner(turned_corner)], axis=0).astype(BF16)

    def put(to_up_ref, to_down_ref):
        to_up_ref[...] = up_ref[...]
        down = jnp.concatenate([bot_ref[...].astype(F32)[: 3 * C], corner(3 * C)], axis=0)
        to_down_ref[...] = down.astype(BF16)

    pl.when(odd == 0)(lambda: put(q1_ref, q2_ref))
    pl.when(odd == 1)(lambda: put(q2_ref, q1_ref))


def turn_edges(fold, west, east, send, bot):
    return pl.pallas_call(
        turn_kernel,
        out_shape=(jax.ShapeDtypeStruct((SWAP, LANES), BF16),) * 2,
        in_specs=[SM] + [VM] * 4,
        out_specs=(VM, VM),
        scratch_shapes=[pltpu.VMEM((SWAP, LANES), BF16)],
        compiler_params=pltpu.CompilerParams(vmem_limit_bytes=10 * 2**20),
    )(fold, west, east, send, bot)


def shifted(full, ends, lane, e):
    s = e - 3
    if s > 0:
        return pltpu.roll(jnp.where(lane < s, ends, full), LANES - s, 1)
    if s < 0:
        return pltpu.roll(jnp.where(lane >= LANES + s, ends, full), -s, 1)
    return full


UNROLL = 5


def conv_kernel(x_ref, band_ref, west_ref, east_ref, y_ref, side_ref):
    lane = lanes_bf16(MAIN)
    tile_lane = lax.broadcasted_iota(jnp.int32, (ROWS, LANES), 1)
    for q in range(13):
        both = jnp.where(
            (tile_lane & 7) < 3,
            west_ref[16 * q : 16 * q + 16, :].astype(F32),
            east_ref[16 * q : 16 * q + 16, :].astype(F32),
        ).astype(BF16)
        for c in range(16 if q < 12 else 8):
            side_ref[16 * q + c] = pltpu.roll(both, LANES - (8 * c + 3), 1)

    def some(t, carry):
        for u in range(UNROLL):
            g = UNROLL * t + u
            full = x_ref[pl.ds(8 * g, 8)].reshape(MAIN, LANES)
            ends = side_ref[pl.ds(8 * g, 8)].reshape(MAIN, LANES)
            rhs = jnp.concatenate([shifted(full, ends, lane, e) for e in range(7)], axis=0)
            y_ref[:, g] = dot32(band_ref[g], rhs).reshape(ROWS, 8, LANES)
        return carry

    lax.fori_loop(0, GROUPS // UNROLL, some, 0)


def conv_own(x, band, west, east):
    return pl.pallas_call(
        conv_kernel,
        out_shape=jax.ShapeDtypeStruct((ROWS, GROUPS, 8, LANES), F32),
        in_specs=[VM] * 4,
        out_specs=VM,
        scratch_shapes=[
            pltpu.VMEM((C, ROWS, LANES), BF16),
        ],
        compiler_params=pltpu.CompilerParams(vmem_limit_bytes=20 * 2**20),
        cost_estimate=pl.CostEstimate(flops=2 * 25 * 256 * 256 * 1024, bytes_accessed=9_000_000, transcendentals=0),
    )(x, band, west, east)


def gelu(h):
    return h * (0.5 + 0.5 * lax.erf(h * np.float32(0.5**0.5)))


def block_kernel(last, block, x_ref, y_ref, band_ref, r1_ref, r2_ref, w1_ref, w2_ref, gain_ref, mask_ref,
                 out_ref, *refs):
    edge_refs, (r32_ref, c32_ref, add_ref, o_ref) = refs[:-4], refs[-4:]
    odd = place_on_mesh()[1]

    def put(below_ref, above_ref):
        for base, ref in ((0, below_ref), (3, above_ref)):
            v = ref[...].astype(F32)
            for k in range(3):
                r32_ref[base + k] = v[k * C : (k + 1) * C].reshape(GROUPS, 8, LANES)
                for q in range(C // PACK):
                    corner = pltpu.roll(v[3 * C :], LANES - (24 * q + 8 * k + 3), 1)
                    c32_ref[base + k, 5 * q : 5 * q + 5] = corner.reshape(5, 8, LANES)

    pl.when(odd == 0)(lambda: put(r2_ref, r1_ref))
    pl.when(odd == 1)(lambda: put(r1_ref, r2_ref))
    lane = lanes_bf16(SIDE)

    def halo(g, carry):
        full = r32_ref[:, g].reshape(SIDE, LANES).astype(BF16)
        ends = c32_ref[:, g].reshape(SIDE, LANES).astype(BF16)
        rhs = jnp.concatenate([shifted(full, ends, lane, e) for e in range(7)], axis=0)
        add_ref[:, g] = dot32(band_ref[g], rhs).reshape(6, 8, LANES)
        return carry

    lax.fori_loop(0, GROUPS, halo, 0, unroll=25)

    def mlp(i0, edges):
        parts = []
        for r in range(2):
            y = y_ref[i0 + r].reshape(C, LANES)
            if edges[r] is not None:
                y = y + add_ref[edges[r]].reshape(C, LANES)
            mean = jnp.sum(y, axis=0, keepdims=True) * np.float32(1 / C)
            y = y - mean
            var = jnp.sum(y * y, axis=0, keepdims=True) * np.float32(1 / C)
            parts.append((y * lax.rsqrt(var + EPS) * gain_ref[...]).astype(BF16))
        hidden = gelu(dot32(w1_ref[...], jnp.concatenate(parts, axis=1))).astype(BF16)
        o = dot32(w2_ref[block], hidden)
        for r in range(2):
            o_ref[pl.ds(i0 + r, C, stride=ROWS), :] = o[:, r * LANES : (r + 1) * LANES]

    edge_of = {row: n for n, row in enumerate(EDGE_ROWS)}
    for i in range(0, ROWS, 2):
        mlp(i, (edge_of.get(i), edge_of.get(i + 1)))
    mask = mask_ref[...]

    def tile(first, count):
        o = o_ref[pl.ds(first * ROWS, count * ROWS), :].reshape(count, ROWS, LANES)
        return (x_ref[pl.ds(first, count)].astype(F32) + o) * mask[None]

    if last:
        def finish(g, carry):
            out_ref[pl.ds(8 * g, 8)] = tile(pl.multiple_of(8 * g, 8), 8).astype(BF16)
            return carry

        lax.fori_loop(0, GROUPS, finish, 0)
    else:
        emit_edges(tile, o_ref, out_ref, *edge_refs)


def run_block(last, block, x, y, band, r1, r2, w1, w2, gain, mask):
    state = jax.ShapeDtypeStruct((C, ROWS, LANES), BF16)
    shapes = (state,) if last else (state,) + EDGE_SHAPES
    return pl.pallas_call(
        lambda *refs: block_kernel(last, block, *refs),
        out_shape=shapes,
        in_specs=[VM] * 9,
        out_specs=(VM,) * len(shapes),
        scratch_shapes=[
            pltpu.VMEM((6, GROUPS, 8, LANES), F32),
            pltpu.VMEM((6, GROUPS, 8, LANES), F32),
            pltpu.VMEM((6, GROUPS, 8, LANES), F32),
            pltpu.VMEM((C * ROWS, LANES), F32),
        ],
        compiler_params=pltpu.CompilerParams(vmem_limit_bytes=20 * 2**20),
    )(x, y, band, r1, r2, w1, w2, gain, mask)


def local(field, land_mask, fold_partner, dw_kernel, norm_gain, w_in, w_out):
    zonal = lax.axis_size("zonal")
    merid = lax.axis_size("merid")
    total = fold_partner.shape[0]
    start = jnp.mod(fold_partner[0] - (LANES // 2 - 1), total)
    turn = start // LANES
    place = lambda m, z: z * merid + m
    even_pairs = [(m, m ^ 1) for m in range(merid)]
    odd_pairs = [(m, ((m - 1) ^ 1) + 1) for m in range(1, merid - 1)]

    def branch_of(shift):
        def branch(q2, mask, *kept):
            pairs = [(place(m, z), place(n, z)) for m, n in odd_pairs for z in range(zonal)]
            pairs += [(place(merid - 1, z), place(merid - 1, (shift - z) % zonal)) for z in range(zonal)]
            return lax.ppermute(q2, ("zonal", "merid"), pairs), float_mask(mask, *kept)

        return branch

    branches = [branch_of(t) for t in range(zonal)]
    taps = jnp.transpose(dw_kernel, (0, 2, 3, 1))
    w2 = jnp.swapaxes(w_out, 1, 2)
    x = field
    send, bot = first_edges(x)
    for b in range(BLOCKS):
        west = lax.ppermute(send, "zonal", [(z, (z + 1) % zonal) for z in range(zonal)])
        east = lax.ppermute(send, "zonal", [((z + 1) % zonal, z) for z in range(zonal)])
        band_main, band_side, w1, gain = make_bands(b, taps, w_in, norm_gain)
        q1, q2 = turn_edges(fold_partner, west, east, send, bot)
        r1 = lax.ppermute(q1, "merid", even_pairs)
        y = conv_own(x, band_main, west, east)
        q2, y = lax.optimization_barrier((q2, y))
        r2, mask = lax.switch(turn, branches, q2, land_mask, x, y, band_side, w1, gain)
        last = b == BLOCKS - 1
        x, *edges = run_block(last, b, x, y, band_side, r1, r2, w1, w2, gain, mask)
        if not last:
            send, bot = edges
    return x


def mask_kernel(mask_ref, *refs):
    out_ref = refs[-1]
    out_ref[...] = mask_ref[...].astype(F32)


def float_mask(mask, *kept):
    return pl.pallas_call(
        mask_kernel,
        out_shape=jax.ShapeDtypeStruct((ROWS, LANES), F32),
        in_specs=[VM] + [pl.BlockSpec(memory_space=pl.ANY)] * len(kept),
        out_specs=VM,
        compiler_params=pltpu.CompilerParams(vmem_limit_bytes=4 * 2**20),
    )(mask, *kept)


def solution(mesh):
    in_specs = (P(None, "merid", "zonal"), P("merid", "zonal"), P(), P(), P(), P(), P())
    out_specs = P(None, "merid", "zonal")
    return jax.shard_map(local, mesh=mesh, in_specs=in_specs, out_specs=out_specs, check_vma=False)
```

profile of v0, /device:TPU:6, one launch (start us, length us, event | category | flops | bytes accessed | tf_op | source)
XLA Modules:
  0.0 101.7 jit_solution(230766985575150060)
XLA Ops:
  0.0 1.7 %shard_map.73 = (bf16[896,128]{1,0:T(8,128)(2,1)S(1)}, bf16[608,128]{1,0:T(8,128)(2,1)S(1)}) custom-call(bf16[200,16,128]{2,1,0:T(8,128)(2,1)} %refs_0_.1), custom_call_target="tpu_custom_call" | custom-call | tf_op jit(solution)/shard_map/pallas_call | solution.py:155
  1.8 3.9 %collective-permute-start.49 = (bf16[896,128]{1,0:T(8,128)(2,1)S(1)}, bf16[896,128]{1,0:T(8,128)(2,1)S(1)}, u32[]{:S(2)}, u32[]{:S(2)}) collective-permute-start(bf16[896,128]{1,0:T(8,128)(2,1)S(1)} %get-tuple-element.1051.send_ref), channel_id=1, source_target_pairs={{8,0},{16,8},{24,16},{32,24},{40,32},{48,40},{56,48},{64,56},{72,6... | collective-permute-start | bytes 688136 | tf_op jit(solution)/shard_map/ppermute | solution.py:383
  5.7 1.2 %slice.3 = s32[1]{0:T(128)} slice(s32[2048]{0:T(1024)} %fold_ref.5), slice={[0:1]} | slice | bytes 8 | tf_op jit(solution)/shard_map/slice | solution.py:362
  7.6 1.2 %copy-done.2 = bf16[3,200,800]{2,1,0:T(8,128)(2,1)S(1)} copy-done((bf16[3,200,800]{2,1,0:T(8,128)(2,1)S(1)}, bf16[3,200,800]{2,1,0:T(8,128)(2,1)}, u32[]{:S(2)}) %copy-start.2) | copy-done | bytes 960024
  8.8 0.9 copy-done.4
  9.7 0.7 copy-done.6
  10.4 3.6 %shard_map.75 = (bf16[25,128,896]{2,1,0:T(8,128)(2,1)S(1)}, bf16[25,48,336]{2,1,0:T(8,128)(2,1)S(1)}, bf16[800,200]{1,0:T(8,128)(2,1)S(1)}, f32[200,128]{1,0:T(8,128)S(1)}) custom-call(bf16[3,7,7,200]{3,2,1,0:T(8,128)(2,1)S(1)} %bitcast.6, bf16[3,200,800]{2,1,0:T(8,128)(2,1)S(1)} %copy-done.2, bf16[3,200]{1,0:T(4,128)(2,1)S(1)} %copy-done.6), custom_call_target="tpu_custom_call" | custom-call | flops 2147483648 | bytes 9000000 | tf_op jit(solution)/shard_map/pallas_call | solution.py:96
  14.0 0.8 shard_map.74
  14.8 4.6 %collective-permute-start.50 = (bf16[640,128]{1,0:T(8,128)(2,1)S(1)}, bf16[640,128]{1,0:T(8,128)(2,1)S(1)}, u32[]{:S(2)}, u32[]{:S(2)}) collective-permute-start(bf16[640,128]{1,0:T(8,128)(2,1)S(1)} %get-tuple-element.1057), channel_id=1, source_target_pairs={{0,1},{1,0},{2,3},{3,2},{4,5},{5,4},{6,7},{7,6},{8,9},{9,8},{10,11... | collective-permute-start | bytes 491528 | tf_op jit(solution)/shard_map/ppermute | solution.py:386
  19.5 4.1 %shard_map.76.refs_1_ = f32[16,25,8,128]{3,2,1,0:T(8,128)} custom-call(bf16[200,16,128]{2,1,0:T(8,128)(2,1)S(1)} %copy-done.9, bf16[25,128,896]{2,1,0:T(8,128)(2,1)S(1)} %get-tuple-element.1054.band_ref, bf16[896,128]{1,0:T(8,128)(2,1)S(1)} %collective-permute-done.48.west_ref, bf16[896,128]{1,0:T(8,128)(2,1)S(1)} %collective-permute-done.49.east_ref), custom_call_target="tpu_custom_call" | custom-call | flops 3355443200 | bytes 9000000 | tf_op jit(solution)/shard_map/pallas_call | solution.py:262
  23.6 9.9 %conditional.3 = (bf16[640,128]{1,0:T(8,128)(2,1)}, f32[16,128]{1,0:T(8,128)S(1)}) conditional(s32[]{:T(128)} %clamp.2, (bf16[640,128]{1,0:T(8,128)(2,1)S(1)}, s32[16,128]{1,0:T(8,128)S(1)}, bf16[200,16,128]{2,1,0:T(8,128)(2,1)S(1)}, f32[16,25,8,128]{3,2,1,0:T(8,128)}, bf16[25,48,336]{2,1,0:T(8,128)(2,1)S(1)}, ...), branch_computations={%region_0.1_spmd, %region_1.2_spmd, %region_2.3_spmd, %region_3.4_... | conditional | bytes 655416 | solution.py:389
  23.6 2.0 %collective-permute-start.10 = (bf16[640,128]{1,0:T(8,128)(2,1)S(1)}, bf16[640,128]{1,0:T(8,128)(2,1)}, u32[]{:S(2)}, u32[]{:S(2)}) collective-permute-start(bf16[640,128]{1,0:T(8,128)(2,1)S(1)} %get-tuple-element.747), channel_id=1, source_target_pairs={{1,2},{9,10},{17,18},{25,26},{33,34},{41,42},{49,50},{57,58},{65,6... | collective-permute-start | bytes 491528 | tf_op jit(solution)/shard_map/cond/branch_10_fun/ppermute | solution.py:372
  25.7 7.9 %collective-permute-done.10 = bf16[640,128]{1,0:T(8,128)(2,1)} collective-permute-done((bf16[640,128]{1,0:T(8,128)(2,1)S(1)}, bf16[640,128]{1,0:T(8,128)(2,1)}, u32[]{:S(2)}, u32[]{:S(2)}) %collective-permute-start.10) | collective-permute-done | bytes 163872 | tf_op jit(solution)/shard_map/cond/branch_10_fun/ppermute | solution.py:372
  33.6 6.2 %shard_map.77 = (bf16[200,16,128]{2,1,0:T(8,128)(2,1)S(1)}, bf16[896,128]{1,0:T(8,128)(2,1)S(1)}, bf16[608,128]{1,0:T(8,128)(2,1)S(1)}) custom-call(bf16[200,16,128]{2,1,0:T(8,128)(2,1)} %refs_0_.1, f32[16,25,8,128]{3,2,1,0:T(8,128)} %shard_map.76.refs_1_, bf16[25,48,336]{2,1,0:T(8,128)(2,1)S(1)} %get-tuple-element.1056.refs_2_, ...), custom_call_target="tpu_custom_call" | custom-call | tf_op jit(solution)/shard_map/pallas_call | solution.py:343
  39.9 3.8 %collective-permute-start.52 = (bf16[896,128]{1,0:T(8,128)(2,1)S(1)}, bf16[896,128]{1,0:T(8,128)(2,1)S(1)}, u32[]{:S(2)}, u32[]{:S(2)}) collective-permute-start(bf16[896,128]{1,0:T(8,128)(2,1)S(1)} %get-tuple-element.1064.send_ref), channel_id=1, source_target_pairs={{8,0},{16,8},{24,16},{32,24},{40,32},{48,40},{56,48},{64,56},{72,6... | collective-permute-start | bytes 688136 | tf_op jit(solution)/shard_map/ppermute | solution.py:383
  43.7 3.6 %shard_map.79 = (bf16[25,128,896]{2,1,0:T(8,128)(2,1)S(1)}, bf16[25,48,336]{2,1,0:T(8,128)(2,1)S(1)}, bf16[800,200]{1,0:T(8,128)(2,1)S(1)}, f32[200,128]{1,0:T(8,128)S(1)}) custom-call(bf16[3,7,7,200]{3,2,1,0:T(8,128)(2,1)S(1)} %bitcast.7, bf16[3,200,800]{2,1,0:T(8,128)(2,1)S(1)} %copy-done.3, bf16[3,200]{1,0:T(4,128)(2,1)S(1)} %copy-done.7), custom_call_target="tpu_custom_call" | custom-call | flops 2147483648 | bytes 9000000 | tf_op jit(solution)/shard_map/pallas_call | solution.py:96
  47.4 0.8 shard_map.78
  48.2 0.8 collective-permute-start.53
  49.1 4.1 %shard_map.80.refs_1_ = f32[16,25,8,128]{3,2,1,0:T(8,128)} custom-call(bf16[200,16,128]{2,1,0:T(8,128)(2,1)S(1)} %get-tuple-element.1063.x_ref.refs_0_, bf16[25,128,896]{2,1,0:T(8,128)(2,1)S(1)} %get-tuple-element.1067.band_ref, bf16[896,128]{1,0:T(8,128)(2,1)S(1)} %collective-permute-done.51.west_ref, bf16[896,128]{1,0:T(8,128)(2,1)S(1)} %collective-permute-done.52.east_ref), custom_call_target="tpu_custom_call" | custom-call | flops 3355443200 | bytes 9000000 | tf_op jit(solution)/shard_map/pallas_call | solution.py:262
  53.2 10.3 %conditional.4 = (bf16[640,128]{1,0:T(8,128)(2,1)}, f32[16,128]{1,0:T(8,128)S(1)}) conditional(s32[]{:T(128)} %clamp.2, (bf16[640,128]{1,0:T(8,128)(2,1)S(1)}, s32[16,128]{1,0:T(8,128)S(1)}, bf16[200,16,128]{2,1,0:T(8,128)(2,1)S(1)}, f32[16,25,8,128]{3,2,1,0:T(8,128)}, bf16[25,48,336]{2,1,0:T(8,128)(2,1)S(1)}, ...), branch_computations={%region_16.17_spmd, %region_17.18_spmd, %region_18.19_spmd, %regio... | conditional | bytes 655416 | solution.py:389
  53.2 4.3 %collective-permute-start.26 = (bf16[640,128]{1,0:T(8,128)(2,1)S(1)}, bf16[640,128]{1,0:T(8,128)(2,1)}, u32[]{:S(2)}, u32[]{:S(2)}) collective-permute-start(bf16[640,128]{1,0:T(8,128)(2,1)S(1)} %get-tuple-element.859), channel_id=1, source_target_pairs={{1,2},{9,10},{17,18},{25,26},{33,34},{41,42},{49,50},{57,58},{65,6... | collective-permute-start | bytes 491528 | tf_op jit(solution)/shard_map/cond/branch_10_fun/ppermute | solution.py:372
  57.5 6.0 %collective-permute-done.26 = bf16[640,128]{1,0:T(8,128)(2,1)} collective-permute-done((bf16[640,128]{1,0:T(8,128)(2,1)S(1)}, bf16[640,128]{1,0:T(8,128)(2,1)}, u32[]{:S(2)}, u32[]{:S(2)}) %collective-permute-start.26) | collective-permute-done | bytes 163872 | tf_op jit(solution)/shard_map/cond/branch_10_fun/ppermute | solution.py:372
  63.5 6.1 %shard_map.81 = (bf16[200,16,128]{2,1,0:T(8,128)(2,1)S(1)}, bf16[896,128]{1,0:T(8,128)(2,1)S(1)}, bf16[608,128]{1,0:T(8,128)(2,1)S(1)}) custom-call(bf16[200,16,128]{2,1,0:T(8,128)(2,1)} %copy-done.10, f32[16,25,8,128]{3,2,1,0:T(8,128)} %shard_map.80.refs_1_, bf16[25,48,336]{2,1,0:T(8,128)(2,1)S(1)} %get-tuple-element.1069.refs_2_, ...), custom_call_target="tpu_custom_call" | custom-call | tf_op jit(solution)/shard_map/pallas_call | solution.py:343
  69.7 3.8 %collective-permute-start.55 = (bf16[896,128]{1,0:T(8,128)(2,1)S(1)}, bf16[896,128]{1,0:T(8,128)(2,1)S(1)}, u32[]{:S(2)}, u32[]{:S(2)}) collective-permute-start(bf16[896,128]{1,0:T(8,128)(2,1)S(1)} %get-tuple-element.1077.send_ref), channel_id=1, source_target_pairs={{8,0},{16,8},{24,16},{32,24},{40,32},{48,40},{56,48},{64,56},{72,6... | collective-permute-start | bytes 688136 | tf_op jit(solution)/shard_map/ppermute | solution.py:383
  73.5 3.6 %shard_map.83 = (bf16[25,128,896]{2,1,0:T(8,128)(2,1)S(1)}, bf16[25,48,336]{2,1,0:T(8,128)(2,1)S(1)}, bf16[800,200]{1,0:T(8,128)(2,1)S(1)}, f32[200,128]{1,0:T(8,128)S(1)}) custom-call(bf16[3,7,7,200]{3,2,1,0:T(8,128)(2,1)S(1)} %bitcast.8, bf16[3,200,800]{2,1,0:T(8,128)(2,1)S(1)} %copy-done.3, bf16[3,200]{1,0:T(4,128)(2,1)S(1)} %copy-done.7), custom_call_target="tpu_custom_call" | custom-call | flops 2147483648 | bytes 9000000 | tf_op jit(solution)/shard_map/pallas_call | solution.py:96
  77.2 0.8 shard_map.82
  78.1 3.1 %collective-permute-start.56 = (bf16[640,128]{1,0:T(8,128)(2,1)S(1)}, bf16[640,128]{1,0:T(8,128)(2,1)S(1)}, u32[]{:S(2)}, u32[]{:S(2)}) collective-permute-start(bf16[640,128]{1,0:T(8,128)(2,1)S(1)} %get-tuple-element.1083), channel_id=1, source_target_pairs={{0,1},{1,0},{2,3},{3,2},{4,5},{5,4},{6,7},{7,6},{8,9},{9,8},{10,11... | collective-permute-start | bytes 491528 | tf_op jit(solution)/shard_map/ppermute | solution.py:386
  81.1 2.9 %shard_map.84.refs_1_ = f32[16,25,8,128]{3,2,1,0:T(8,128)S(1)} custom-call(bf16[200,16,128]{2,1,0:T(8,128)(2,1)S(1)} %get-tuple-element.1076.x_ref.refs_0_, bf16[25,128,896]{2,1,0:T(8,128)(2,1)S(1)} %get-tuple-element.1080.band_ref, bf16[896,128]{1,0:T(8,128)(2,1)S(1)} %collective-permute-done.54.west_ref, bf16[896,128]{1,0:T(8,128)(2,1)S(1)} %collective-permute-done.55.east_ref), custom_call_target="tpu_custom_call" | custom-call | flops 3355443200 | bytes 9000000 | tf_op jit(solution)/shard_map/pallas_call | solution.py:262
  84.1 11.1 %conditional.5 = (bf16[640,128]{1,0:T(8,128)(2,1)}, f32[16,128]{1,0:T(8,128)S(1)}) conditional(s32[]{:T(128)} %clamp.2, (bf16[640,128]{1,0:T(8,128)(2,1)S(1)}, s32[16,128]{1,0:T(8,128)S(1)}, bf16[200,16,128]{2,1,0:T(8,128)(2,1)S(1)}, f32[16,25,8,128]{3,2,1,0:T(8,128)S(1)}, bf16[25,48,336]{2,1,0:T(8,128)(2,1)S(1)}, ...), branch_computations={%region_32.33_spmd, %region_33.34_spmd, %region_34.35_spmd, %regio... | conditional | bytes 655416 | solution.py:389
  84.1 1.9 %collective-permute-start.42 = (bf16[640,128]{1,0:T(8,128)(2,1)S(1)}, bf16[640,128]{1,0:T(8,128)(2,1)}, u32[]{:S(2)}, u32[]{:S(2)}) collective-permute-start(bf16[640,128]{1,0:T(8,128)(2,1)S(1)} %get-tuple-element.971), channel_id=1, source_target_pairs={{1,2},{9,10},{17,18},{25,26},{33,34},{41,42},{49,50},{57,58},{65,6... | collective-permute-start | bytes 491528 | tf_op jit(solution)/shard_map/cond/branch_10_fun/ppermute | solution.py:372
  86.1 9.1 %collective-permute-done.42 = bf16[640,128]{1,0:T(8,128)(2,1)} collective-permute-done((bf16[640,128]{1,0:T(8,128)(2,1)S(1)}, bf16[640,128]{1,0:T(8,128)(2,1)}, u32[]{:S(2)}, u32[]{:S(2)}) %collective-permute-start.42) | collective-permute-done | bytes 163872 | tf_op jit(solution)/shard_map/cond/branch_10_fun/ppermute | solution.py:372
  95.2 6.5 %shard_map.85 = bf16[200,16,128]{2,1,0:T(8,128)(2,1)} custom-call(bf16[200,16,128]{2,1,0:T(8,128)(2,1)} %copy-done.11, f32[16,25,8,128]{3,2,1,0:T(8,128)S(1)} %shard_map.84.refs_1_, bf16[25,48,336]{2,1,0:T(8,128)(2,1)} %copy-done.8, bf16[640,128]{1,0:T(8,128)(2,1)S(1)} %collective-permute-done.56.refs_3_, bf16[640,128]{1,0:T(8,128)(2,1)} %get-tuple-element.1087.refs_4_, ...), custom_call_target="tpu_custom_call" | custom-call | tf_op jit(solution)/shard_map/pallas_call | solution.py:343
  (46 shorter events, 0.5 us)
Async XLA Ops:
  1.7 12.3 %collective-permute-start.48 = (bf16[896,128]{1,0:T(8,128)(2,1)S(1)}, bf16[896,128]{1,0:T(8,128)(2,1)S(1)}, u32[]{:S(2)}, u32[]{:S(2)}) collective-permute-start(bf16[896,128]{1,0:T(8,128)(2,1)S(1)} %get-tuple-element.1051.send_ref), channel_id=1, source_target_pairs={{0,8},{8,16},{16,24},{24,32},{32,40},{40,48},{48,56},{56,64},{64,7... | collective-permute-start | bytes 688136 | tf_op jit(solution)/shard_map/ppermute | solution.py:382
  1.8 12.2 %collective-permute-start.49 = (bf16[896,128]{1,0:T(8,128)(2,1)S(1)}, bf16[896,128]{1,0:T(8,128)(2,1)S(1)}, u32[]{:S(2)}, u32[]{:S(2)}) collective-permute-start(bf16[896,128]{1,0:T(8,128)(2,1)S(1)} %get-tuple-element.1051.send_ref), channel_id=1, source_target_pairs={{8,0},{16,8},{24,16},{32,24},{40,32},{48,40},{56,48},{64,56},{72,6... | collective-permute-start | bytes 688136 | tf_op jit(solution)/shard_map/ppermute | solution.py:383
  7.6 1.2 %copy-start.2 = (bf16[3,200,800]{2,1,0:T(8,128)(2,1)S(1)}, bf16[3,200,800]{2,1,0:T(8,128)(2,1)}, u32[]{:S(2)}) copy-start(bf16[3,200,800]{2,1,0:T(8,128)(2,1)} %refs_1_.5) | copy-start | bytes 2880004
  8.8 0.9 copy-start.4
  9.7 0.7 copy-start.6
  10.4 3.6 %copy-start.1 = (s32[2048]{0:T(1024)S(1)}, s32[2048]{0:T(1024)}, u32[]{:S(2)}) copy-start(s32[2048]{0:T(1024)} %fold_ref.5) | copy-start | bytes 24580
  10.4 9.1 %copy-start.9 = (bf16[200,16,128]{2,1,0:T(8,128)(2,1)S(1)}, bf16[200,16,128]{2,1,0:T(8,128)(2,1)}, u32[]{:S(2)}) copy-start(bf16[200,16,128]{2,1,0:T(8,128)(2,1)} %refs_0_.1) | copy-start | bytes 2457604
  14.0 9.6 %copy-start.13 = (bf16[800,200]{1,0:T(8,128)(2,1)}, bf16[800,200]{1,0:T(8,128)(2,1)S(1)}, u32[]{:S(2)}) copy-start(bf16[800,200]{1,0:T(8,128)(2,1)S(1)} %get-tuple-element.1059.refs_5_) | copy-start | bytes 960004
  14.8 18.7 %collective-permute-start.50 = (bf16[640,128]{1,0:T(8,128)(2,1)S(1)}, bf16[640,128]{1,0:T(8,128)(2,1)S(1)}, u32[]{:S(2)}, u32[]{:S(2)}) collective-permute-start(bf16[640,128]{1,0:T(8,128)(2,1)S(1)} %get-tuple-element.1057), channel_id=1, source_target_pairs={{0,1},{1,0},{2,3},{3,2},{4,5},{5,4},{6,7},{7,6},{8,9},{9,8},{10,11... | collective-permute-start | bytes 491528 | tf_op jit(solution)/shard_map/ppermute | solution.py:386
  19.5 4.1 %copy-start.15 = (s32[16,128]{1,0:T(8,128)S(1)}, s32[16,128]{1,0:T(8,128)}, u32[]{:S(2)}) copy-start(s32[16,128]{1,0:T(8,128)} %param.56) | copy-start | bytes 24580
  23.6 10.0 %copy-start = (bf16[3,800,200]{1,2,0:T(8,128)(2,1)S(1)}, bf16[3,800,200]{1,2,0:T(8,128)(2,1)}, u32[]{:S(2)}) copy-start(bf16[3,800,200]{1,2,0:T(8,128)(2,1)} %param.61) | copy-start | bytes 2880004
  23.6 9.9 %collective-permute-start.10 = (bf16[640,128]{1,0:T(8,128)(2,1)S(1)}, bf16[640,128]{1,0:T(8,128)(2,1)}, u32[]{:S(2)}, u32[]{:S(2)}) collective-permute-start(bf16[640,128]{1,0:T(8,128)(2,1)S(1)} %get-tuple-element.747), channel_id=1, source_target_pairs={{1,2},{9,10},{17,18},{25,26},{33,34},{41,42},{49,50},{57,58},{65,6... | collective-permute-start | bytes 491528 | tf_op jit(solution)/shard_map/cond/branch_10_fun/ppermute | solution.py:372
  33.5 10.2 %copy-start.3 = (bf16[3,200,800]{2,1,0:T(8,128)(2,1)S(1)}, bf16[3,200,800]{2,1,0:T(8,128)(2,1)}, u32[]{:S(2)}) copy-start(bf16[3,200,800]{2,1,0:T(8,128)(2,1)} %refs_1_.5) | copy-start | bytes 2880004
  33.5 10.2 %copy-start.5 = (bf16[3,200,7,7]{1,3,2,0:T(8,128)(2,1)S(1)}, bf16[3,200,7,7]{1,3,2,0:T(8,128)(2,1)}, u32[]{:S(2)}) copy-start(bf16[3,200,7,7]{1,3,2,0:T(8,128)(2,1)} %param.58) | copy-start | bytes 176404
  33.6 10.2 %copy-start.7 = (bf16[3,200]{1,0:T(4,128)(2,1)S(1)}, bf16[3,200]{1,0:T(4,128)(2,1)}, u32[]{:S(2)}) copy-start(bf16[3,200]{1,0:T(4,128)(2,1)} %refs_2_.5) | copy-start | bytes 3604
  39.8 13.4 %copy-start.10 = (bf16[200,16,128]{2,1,0:T(8,128)(2,1)}, bf16[200,16,128]{2,1,0:T(8,128)(2,1)S(1)}, u32[]{:S(2)}) copy-start(bf16[200,16,128]{2,1,0:T(8,128)(2,1)S(1)} %get-tuple-element.1063.x_ref.refs_0_) | copy-start | bytes 2457604
  39.8 7.6 %collective-permute-start.51 = (bf16[896,128]{1,0:T(8,128)(2,1)S(1)}, bf16[896,128]{1,0:T(8,128)(2,1)S(1)}, u32[]{:S(2)}, u32[]{:S(2)}) collective-permute-start(bf16[896,128]{1,0:T(8,128)(2,1)S(1)} %get-tuple-element.1064.send_ref), channel_id=1, source_target_pairs={{0,8},{8,16},{16,24},{24,32},{32,40},{40,48},{48,56},{56,64},{64,7... | collective-permute-start | bytes 688136 | tf_op jit(solution)/shard_map/ppermute | solution.py:382
  39.9 7.5 %collective-permute-start.52 = (bf16[896,128]{1,0:T(8,128)(2,1)S(1)}, bf16[896,128]{1,0:T(8,128)(2,1)S(1)}, u32[]{:S(2)}, u32[]{:S(2)}) collective-permute-start(bf16[896,128]{1,0:T(8,128)(2,1)S(1)} %get-tuple-element.1064.send_ref), channel_id=1, source_target_pairs={{8,0},{16,8},{24,16},{32,24},{40,32},{48,40},{56,48},{64,56},{72,6... | collective-permute-start | bytes 688136 | tf_op jit(solution)/shard_map/ppermute | solution.py:383
  47.3 5.9 %copy-start.12 = (bf16[800,200]{1,0:T(8,128)(2,1)}, bf16[800,200]{1,0:T(8,128)(2,1)S(1)}, u32[]{:S(2)}) copy-start(bf16[800,200]{1,0:T(8,128)(2,1)S(1)} %get-tuple-element.1072.refs_5_) | copy-start | bytes 960004
  47.3 5.9 %copy-start.14 = (f32[200,128]{1,0:T(8,128)}, f32[200,128]{1,0:T(8,128)S(1)}, u32[]{:S(2)}) copy-start(f32[200,128]{1,0:T(8,128)S(1)} %get-tuple-element.1073.refs_7_) | copy-start | bytes 307204
  48.2 15.3 %collective-permute-start.53 = (bf16[640,128]{1,0:T(8,128)(2,1)S(1)}, bf16[640,128]{1,0:T(8,128)(2,1)S(1)}, u32[]{:S(2)}, u32[]{:S(2)}) collective-permute-start(bf16[640,128]{1,0:T(8,128)(2,1)S(1)} %get-tuple-element.1070), channel_id=1, source_target_pairs={{0,1},{1,0},{2,3},{3,2},{4,5},{5,4},{6,7},{7,6},{8,9},{9,8},{10,11... | collective-permute-start | bytes 491528 | tf_op jit(solution)/shard_map/ppermute | solution.py:386
  53.2 10.3 %collective-permute-start.26 = (bf16[640,128]{1,0:T(8,128)(2,1)S(1)}, bf16[640,128]{1,0:T(8,128)(2,1)}, u32[]{:S(2)}, u32[]{:S(2)}) collective-permute-start(bf16[640,128]{1,0:T(8,128)(2,1)S(1)} %get-tuple-element.859), channel_id=1, source_target_pairs={{1,2},{9,10},{17,18},{25,26},{33,34},{41,42},{49,50},{57,58},{65,6... | collective-permute-start | bytes 491528 | tf_op jit(solution)/shard_map/cond/branch_10_fun/ppermute | solution.py:372
  69.6 14.4 %copy-start.11 = (bf16[200,16,128]{2,1,0:T(8,128)(2,1)}, bf16[200,16,128]{2,1,0:T(8,128)(2,1)S(1)}, u32[]{:S(2)}) copy-start(bf16[200,16,128]{2,1,0:T(8,128)(2,1)S(1)} %get-tuple-element.1076.x_ref.refs_0_) | copy-start | bytes 2457604
  69.6 7.6 %collective-permute-start.54 = (bf16[896,128]{1,0:T(8,128)(2,1)S(1)}, bf16[896,128]{1,0:T(8,128)(2,1)S(1)}, u32[]{:S(2)}, u32[]{:S(2)}) collective-permute-start(bf16[896,128]{1,0:T(8,128)(2,1)S(1)} %get-tuple-element.1077.send_ref), channel_id=1, source_target_pairs={{0,8},{8,16},{16,24},{24,32},{32,40},{40,48},{48,56},{56,64},{64,7... | collective-permute-start | bytes 688136 | tf_op jit(solution)/shard_map/ppermute | solution.py:382
  69.7 7.5 %collective-permute-start.55 = (bf16[896,128]{1,0:T(8,128)(2,1)S(1)}, bf16[896,128]{1,0:T(8,128)(2,1)S(1)}, u32[]{:S(2)}, u32[]{:S(2)}) collective-permute-start(bf16[896,128]{1,0:T(8,128)(2,1)S(1)} %get-tuple-element.1077.send_ref), channel_id=1, source_target_pairs={{8,0},{16,8},{24,16},{32,24},{40,32},{48,40},{56,48},{64,56},{72,6... | collective-permute-start | bytes 688136 | tf_op jit(solution)/shard_map/ppermute | solution.py:383
  77.1 6.9 %copy-start.8 = (bf16[25,48,336]{2,1,0:T(8,128)(2,1)}, bf16[25,48,336]{2,1,0:T(8,128)(2,1)S(1)}, u32[]{:S(2)}) copy-start(bf16[25,48,336]{2,1,0:T(8,128)(2,1)S(1)} %get-tuple-element.1082.refs_2_) | copy-start | bytes 2419204
  78.1 17.1 %collective-permute-start.56 = (bf16[640,128]{1,0:T(8,128)(2,1)S(1)}, bf16[640,128]{1,0:T(8,128)(2,1)S(1)}, u32[]{:S(2)}, u32[]{:S(2)}) collective-permute-start(bf16[640,128]{1,0:T(8,128)(2,1)S(1)} %get-tuple-element.1083), channel_id=1, source_target_pairs={{0,1},{1,0},{2,3},{3,2},{4,5},{5,4},{6,7},{7,6},{8,9},{9,8},{10,11... | collective-permute-start | bytes 491528 | tf_op jit(solution)/shard_map/ppermute | solution.py:386
  81.1 2.9 %copy-start.16 = (s32[16,128]{1,0:T(8,128)S(1)}, s32[16,128]{1,0:T(8,128)}, u32[]{:S(2)}) copy-start(s32[16,128]{1,0:T(8,128)} %param.56) | copy-start | bytes 24580
  84.1 11.1 %collective-permute-start.42 = (bf16[640,128]{1,0:T(8,128)(2,1)S(1)}, bf16[640,128]{1,0:T(8,128)(2,1)}, u32[]{:S(2)}, u32[]{:S(2)}) collective-permute-start(bf16[640,128]{1,0:T(8,128)(2,1)S(1)} %get-tuple-element.971), channel_id=1, source_target_pairs={{1,2},{9,10},{17,18},{25,26},{33,34},{41,42},{49,50},{57,58},{65,6... | collective-permute-start | bytes 491528 | tf_op jit(solution)/shard_map/cond/branch_10_fun/ppermute | solution.py:372
where the time goes:
time: 102 us
  Pallas kernels  44.8 us (44%)
  starting transfers between devices  28.6 us (28%)
  waiting for transfers between devices  23.2 us (23%)
  local copies, waits for them, and re-layouts  4.06 us (4%)
    ppermute x3, waiting for transfers between devices, branch(): lax.ppermute(q2, ('zonal', 'merid'), pairs)  23 us
    pallas_call x3, Pallas kernels, run_block(): pl.pallas_call(lambda *refs: block_kernel(last, block, *refs), out_shape=...  18.8 us
    ppermute x3, starting transfers between devices, local(): lax.ppermute(send, 'zonal', [((z + 1) % zonal, z) for z in range(zonal)])  11.6 us
    pallas_call x3, Pallas kernels, conv_own(): pl.pallas_call(conv_kernel, out_shape=jax.ShapeDtypeStruct((ROWS, GROUPS,...  11.1 us
    pallas_call x3, Pallas kernels, make_bands(): pl.pallas_call(lambda *refs: band_kernel(block, *refs), out_shape=(jax.Sh...  10.7 us
    ppermute x3, starting transfers between devices, local(): r1 = lax.ppermute(q1, 'merid', even_pairs)  8.55 us
    ppermute x3, starting transfers between devices, branch(): lax.ppermute(q2, ('zonal', 'merid'), pairs)  8.29 us
    unnamed x34, local copies, waits for them, and re-layouts  2.86 us
  transfers between devices with their start and end apart: 12, of which 5 were waited for; matrix products, arithmetic and copies ran while one was open for 1% of the time, Pallas kernels for 21%

commit v1 on v0

--- a/solution.py
+++ b/solution.py
@@ -103,7 +103,7 @@
         ),
         in_specs=[VM] * 3,
         out_specs=(VM,) * 4,
-        compiler_params=pltpu.CompilerParams(vmem_limit_bytes=20 * 2**20),
+        compiler_params=pltpu.CompilerParams(vmem_limit_bytes=14 * 2**20),
         cost_estimate=pl.CostEstimate(flops=2 * 16 * 256 * 256 * 1024, bytes_accessed=9_000_000, transcendentals=0),
     )(taps, w_in, gain)
 
@@ -158,7 +158,7 @@
         in_specs=[VM],
         out_specs=(VM,) * 2,
         scratch_shapes=[pltpu.VMEM((C * ROWS, LANES), F32)],
-        compiler_params=pltpu.CompilerParams(vmem_limit_bytes=10 * 2**20),
+        compiler_params=pltpu.CompilerParams(vmem_limit_bytes=6 * 2**20),
     )(x)
 
 
@@ -218,7 +218,7 @@
         in_specs=[SM] + [VM] * 4,
         out_specs=(VM, VM),
         scratch_shapes=[pltpu.VMEM((SWAP, LANES), BF16)],
-        compiler_params=pltpu.CompilerParams(vmem_limit_bytes=10 * 2**20),
+        compiler_params=pltpu.CompilerParams(vmem_limit_bytes=6 * 2**20),
     )(fold, west, east, send, bot)
 
 
@@ -267,7 +267,7 @@
         scratch_shapes=[
             pltpu.VMEM((C, ROWS, LANES), BF16),
         ],
-        compiler_params=pltpu.CompilerParams(vmem_limit_bytes=20 * 2**20),
+        compiler_params=pltpu.CompilerParams(vmem_limit_bytes=14 * 2**20),
         cost_estimate=pl.CostEstimate(flops=2 * 25 * 256 * 256 * 1024, bytes_accessed=9_000_000, transcendentals=0),
     )(x, band, west, east)
 
@@ -276,10 +276,10 @@
     return h * (0.5 + 0.5 * lax.erf(h * np.float32(0.5**0.5)))
 
 
-def block_kernel(last, block, x_ref, y_ref, band_ref, r1_ref, r2_ref, w1_ref, w2_ref, gain_ref, mask_ref,
+def block_kernel(last, block, x_ref, y_ref, band_ref, r1_ref, r2_ref, r3_ref, w1_ref, w2_ref, gain_ref, mask_ref,
                  out_ref, *refs):
     edge_refs, (r32_ref, c32_ref, add_ref, o_ref) = refs[:-4], refs[-4:]
-    odd = place_on_mesh()[1]
+    at_top, odd = place_on_mesh()
 
     def put(below_ref, above_ref):
         for base, ref in ((0, below_ref), (3, above_ref)):
@@ -291,7 +291,8 @@
                     c32_ref[base + k, 5 * q : 5 * q + 5] = corner.reshape(5, 8, LANES)
 
     pl.when(odd == 0)(lambda: put(r2_ref, r1_ref))
-    pl.when(odd == 1)(lambda: put(r1_ref, r2_ref))
+    pl.when((odd == 1) & jnp.logical_not(at_top))(lambda: put(r1_ref, r2_ref))
+    pl.when(at_top)(lambda: put(r1_ref, r3_ref))
     lane = lanes_bf16(SIDE)
 
     def halo(g, carry):
@@ -337,13 +338,13 @@
         emit_edges(tile, o_ref, out_ref, *edge_refs)
 
 
-def run_block(last, block, x, y, band, r1, r2, w1, w2, gain, mask):
+def run_block(last, block, x, y, band, r1, r2, r3, w1, w2, gain, mask):
     state = jax.ShapeDtypeStruct((C, ROWS, LANES), BF16)
     shapes = (state,) if last else (state,) + EDGE_SHAPES
     return pl.pallas_call(
         lambda *refs: block_kernel(last, block, *refs),
         out_shape=shapes,
-        in_specs=[VM] * 9,
+        in_specs=[VM] * 10,
         out_specs=(VM,) * len(shapes),
         scratch_shapes=[
             pltpu.VMEM((6, GROUPS, 8, LANES), F32),
@@ -351,8 +352,8 @@
             pltpu.VMEM((6, GROUPS, 8, LANES), F32),
             pltpu.VMEM((C * ROWS, LANES), F32),
         ],
-        compiler_params=pltpu.CompilerParams(vmem_limit_bytes=20 * 2**20),
-    )(x, y, band, r1, r2, w1, w2, gain, mask)
+        compiler_params=pltpu.CompilerParams(vmem_limit_bytes=14 * 2**20),
+    )(x, y, band, r1, r2, r3, w1, w2, gain, mask)
 
 
 def local(field, land_mask, fold_partner, dw_kernel, norm_gain, w_in, w_out):
@@ -366,10 +367,9 @@
     odd_pairs = [(m, ((m - 1) ^ 1) + 1) for m in range(1, merid - 1)]
 
     def branch_of(shift):
-        def branch(q2, mask, *kept):
-            pairs = [(place(m, z), place(n, z)) for m, n in odd_pairs for z in range(zonal)]
-            pairs += [(place(merid - 1, z), place(merid - 1, (shift - z) % zonal)) for z in range(zonal)]
-            return lax.ppermute(q2, ("zonal", "merid"), pairs), float_mask(mask, *kept)
+        def branch(rows, mask, *kept):
+            pairs = [(place(merid - 1, z), place(merid - 1, (shift - z) % zonal)) for z in range(zonal)]
+            return lax.ppermute(rows, ("zonal", "merid"), pairs), float_mask(mask, *kept)
 
         return branch
 
@@ -384,11 +384,12 @@
         band_main, band_side, w1, gain = make_bands(b, taps, w_in, norm_gain)
         q1, q2 = turn_edges(fold_partner, west, east, send, bot)
         r1 = lax.ppermute(q1, "merid", even_pairs)
+        r2 = lax.ppermute(q2, "merid", odd_pairs)
         y = conv_own(x, band_main, west, east)
         q2, y = lax.optimization_barrier((q2, y))
-        r2, mask = lax.switch(turn, branches, q2, land_mask, x, y, band_side, w1, gain)
+        r3, mask = lax.switch(turn, branches, q2, land_mask, x, y, band_side, w1, gain)
         last = b == BLOCKS - 1
-        x, *edges = run_block(last, b, x, y, band_side, r1, r2, w1, w2, gain, mask)
+        x, *edges = run_block(last, b, x, y, band_side, r1, r2, r3, w1, w2, gain, mask)
         if not last:
             send, bot = edges
     return x

time: 102 us -> 99 us (0.971)
  waiting for transfers between devices: 23.2 us -> 10.2 us
  starting transfers between devices: 28.6 us -> 36.3 us
  Pallas kernels: 44.8 us -> 47.1 us
    ppermute x3 -> x6, waiting for transfers between devices: 23 us -> 9.97 us  [the longest x3 9.97 us: local(): r2 = lax.ppermute(q2, 'merid', odd_pairs)]
    ppermute x3, starting transfers between devices: 8.55 us -> 14.6 us  [local(): r1 = lax.ppermute(q1, 'merid', even_pairs)]
    pallas_call x3, Pallas kernels: 2.43 us -> 4.6 us  [turn_edges(): pl.pallas_call(turn_kernel, out_shape=(jax.ShapeDtypeStruct((SWAP, LANES)...]
    ppermute x3 -> x6, starting transfers between devices: 8.29 us -> 9.86 us  [the longest x3 5.72 us: local(): r2 = lax.ppermute(q2, 'merid', odd_pairs)]
  transfers between devices with their start and end apart: 12 -> 15, of which waited for: 5 -> 5; matrix products, arithmetic and copies ran while one was open for 1% -> 1% of each run, Pallas kernels for 21% -> 22%
where the time goes in v1:
time: 99 us; the launch traced here: 98.9 us
  Pallas kernels  47.1 us (48%)
  starting transfers between devices  36.3 us (37%)
  waiting for transfers between devices  10.2 us (10%)
  local copies, waits for them, and re-layouts  4.05 us (4%)
    pallas_call x3, Pallas kernels, run_block(): pl.pallas_call(lambda *refs: block_kernel(last, block, *refs), out_shape=...  19 us
    ppermute x3, starting transfers between devices, local(): r1 = lax.ppermute(q1, 'merid', even_pairs)  14.6 us
    ppermute x3, starting transfers between devices, local(): lax.ppermute(send, 'zonal', [((z + 1) % zonal, z) for z in range(zonal)])  11.6 us
    pallas_call x3, Pallas kernels, conv_own(): pl.pallas_call(conv_kernel, out_shape=jax.ShapeDtypeStruct((ROWS, GROUPS,...  11.1 us
    pallas_call x3, Pallas kernels, make_bands(): pl.pallas_call(lambda *refs: band_kernel(block, *refs), out_shape=(jax.Sh...  10.7 us
    ppermute x3, waiting for transfers between devices, local(): r2 = lax.ppermute(q2, 'merid', odd_pairs)  9.97 us
    ppermute x3, starting transfers between devices, local(): r2 = lax.ppermute(q2, 'merid', odd_pairs)  5.72 us
    pallas_call x3, Pallas kernels, turn_edges(): pl.pallas_call(turn_kernel, out_shape=(jax.ShapeDtypeStruct((SWAP, LANES)...  4.6 us
  transfers between devices with their start and end apart: 15, of which 5 were waited for; matrix products, arithmetic and copies ran while one was open for 1% of the time, Pallas kernels for 22%

profile of v1, /device:TPU:6, one launch (start us, length us, event | category | flops | bytes accessed | tf_op | source)
XLA Modules:
  0.0 98.9 jit_solution(16119471700213860290)
XLA Ops:
  0.0 1.7 %shard_map.73 = (bf16[896,128]{1,0:T(8,128)(2,1)S(1)}, bf16[608,128]{1,0:T(8,128)(2,1)S(1)}) custom-call(bf16[200,16,128]{2,1,0:T(8,128)(2,1)} %refs_0_.1), custom_call_target="tpu_custom_call" | custom-call | tf_op jit(solution)/shard_map/pallas_call | solution.py:155
  1.8 3.9 %collective-permute-start.49 = (bf16[896,128]{1,0:T(8,128)(2,1)S(1)}, bf16[896,128]{1,0:T(8,128)(2,1)S(1)}, u32[]{:S(2)}, u32[]{:S(2)}) collective-permute-start(bf16[896,128]{1,0:T(8,128)(2,1)S(1)} %get-tuple-element.1051.send_ref), channel_id=1, source_target_pairs={{8,0},{16,8},{24,16},{32,24},{40,32},{48,40},{56,48},{64,56},{72,6... | collective-permute-start | bytes 688136 | tf_op jit(solution)/shard_map/ppermute | solution.py:383
  7.6 1.2 %copy-done.2 = bf16[3,200,800]{2,1,0:T(8,128)(2,1)S(1)} copy-done((bf16[3,200,800]{2,1,0:T(8,128)(2,1)S(1)}, bf16[3,200,800]{2,1,0:T(8,128)(2,1)}, u32[]{:S(2)}) %copy-start.2) | copy-done | bytes 960024
  10.4 3.6 %shard_map.75 = (bf16[25,128,896]{2,1,0:T(8,128)(2,1)S(1)}, bf16[25,48,336]{2,1,0:T(8,128)(2,1)S(1)}, bf16[800,200]{1,0:T(8,128)(2,1)S(1)}, f32[200,128]{1,0:T(8,128)S(1)}) custom-call(bf16[3,7,7,200]{3,2,1,0:T(8,128)(2,1)S(1)} %bitcast.6, bf16[3,200,800]{2,1,0:T(8,128)(2,1)S(1)} %copy-done.2, bf16[3,200]{1,0:T(4,128)(2,1)S(1)} %copy-done.6), custom_call_target="tpu_custom_call" | custom-call | flops 2147483648 | bytes 9000000 | tf_op jit(solution)/shard_map/pallas_call | solution.py:96
  14.0 1.5 %shard_map.74 = (bf16[640,128]{1,0:T(8,128)(2,1)S(1)}, bf16[640,128]{1,0:T(8,128)(2,1)}) custom-call(s32[2048]{0:T(1024)S(1)} %copy-done.1, bf16[896,128]{1,0:T(8,128)(2,1)S(1)} %collective-permute-done.48.west_ref, bf16[896,128]{1,0:T(8,128)(2,1)S(1)} %collective-permute-done.49.east_ref, bf16[896,128]{1,0:T(8,128)(2,1)S(1)} %get-tuple-element.1051.send_ref, ...), custom_call_target="tpu_custom_call" | custom-call | tf_op jit(solution)/shard_map/pallas_call | solution.py:215
  15.5 4.6 %collective-permute-start.50 = (bf16[640,128]{1,0:T(8,128)(2,1)S(1)}, bf16[640,128]{1,0:T(8,128)(2,1)S(1)}, u32[]{:S(2)}, u32[]{:S(2)}) collective-permute-start(bf16[640,128]{1,0:T(8,128)(2,1)S(1)} %get-tuple-element.1057), channel_id=1, source_target_pairs={{0,1},{1,0},{2,3},{3,2},{4,5},{5,4},{6,7},{7,6},{8,9},{9,8},{10,11... | collective-permute-start | bytes 491528 | tf_op jit(solution)/shard_map/ppermute | solution.py:386
  20.1 1.9 %collective-permute-start.51 = (bf16[640,128]{1,0:T(8,128)(2,1)}, bf16[640,128]{1,0:T(8,128)(2,1)S(1)}, u32[]{:S(2)}, u32[]{:S(2)}) collective-permute-start(bf16[640,128]{1,0:T(8,128)(2,1)} %get-tuple-element.1058), channel_id=1, source_target_pairs={{1,2},{2,1},{3,4},{4,3},{5,6},{6,5},{9,10},{10,9},{11,12},{12,11},... | collective-permute-start | bytes 491528 | tf_op jit(solution)/shard_map/ppermute | solution.py:387
  22.0 4.1 %shard_map.76.refs_1_ = f32[16,25,8,128]{3,2,1,0:T(8,128)} custom-call(bf16[200,16,128]{2,1,0:T(8,128)(2,1)S(1)} %copy-done.10, bf16[25,128,896]{2,1,0:T(8,128)(2,1)S(1)} %get-tuple-element.1054.band_ref, bf16[896,128]{1,0:T(8,128)(2,1)S(1)} %collective-permute-done.48.west_ref, bf16[896,128]{1,0:T(8,128)(2,1)S(1)} %collective-permute-done.49.east_ref), custom_call_target="tpu_custom_call" | custom-call | flops 3355443200 | bytes 9000000 | tf_op jit(solution)/shard_map/pallas_call | solution.py:262
  26.1 1.5 %conditional.3 = (bf16[640,128]{1,0:T(8,128)(2,1)}, f32[16,128]{1,0:T(8,128)S(1)}) conditional(s32[]{:T(128)} %clamp.2, (bf16[640,128]{1,0:T(8,128)(2,1)}, s32[16,128]{1,0:T(8,128)S(1)}, bf16[200,16,128]{2,1,0:T(8,128)(2,1)S(1)}, f32[16,25,8,128]{3,2,1,0:T(8,128)}, bf16[25,48,336]{2,1,0:T(8,128)(2,1)S(1)}, ...), branch_computations={%region_0.1_spmd, %region_1.2_spmd, %region_2.3_spmd, %region_3.4_... | conditional | bytes 655416 | solution.py:390
  26.2 1.5 %collective-permute-start.15 = (bf16[640,128]{1,0:T(8,128)(2,1)}, bf16[640,128]{1,0:T(8,128)(2,1)}, u32[]{:S(2)}, u32[]{:S(2)}) collective-permute-start(bf16[640,128]{1,0:T(8,128)(2,1)} %get-tuple-element.782), channel_id=1, source_target_pairs={{7,127},{15,119},{23,111},{31,103},{39,95},{47,87},{55,79},{63,71}... | collective-permute-start | bytes 491528 | tf_op jit(solution)/shard_map/cond/branch_15_fun/ppermute | solution.py:372
  27.7 2.2 %collective-permute-done.51.refs_4_ = bf16[640,128]{1,0:T(8,128)(2,1)S(1)} collective-permute-done((bf16[640,128]{1,0:T(8,128)(2,1)}, bf16[640,128]{1,0:T(8,128)(2,1)S(1)}, u32[]{:S(2)}, u32[]{:S(2)}) %collective-permute-start.51) | collective-permute-done | bytes 163872 | tf_op jit(solution)/shard_map/ppermute | solution.py:387
  29.9 6.2 %shard_map.77 = (bf16[200,16,128]{2,1,0:T(8,128)(2,1)S(1)}, bf16[896,128]{1,0:T(8,128)(2,1)S(1)}, bf16[608,128]{1,0:T(8,128)(2,1)S(1)}) custom-call(bf16[200,16,128]{2,1,0:T(8,128)(2,1)} %refs_0_.1, f32[16,25,8,128]{3,2,1,0:T(8,128)} %shard_map.76.refs_1_, bf16[25,48,336]{2,1,0:T(8,128)(2,1)S(1)} %get-tuple-element.1056.refs_2_, ...), custom_call_target="tpu_custom_call" | custom-call | tf_op jit(solution)/shard_map/pallas_call | solution.py:344
  36.2 3.8 %collective-permute-start.53 = (bf16[896,128]{1,0:T(8,128)(2,1)S(1)}, bf16[896,128]{1,0:T(8,128)(2,1)S(1)}, u32[]{:S(2)}, u32[]{:S(2)}) collective-permute-start(bf16[896,128]{1,0:T(8,128)(2,1)S(1)} %get-tuple-element.1064.send_ref), channel_id=1, source_target_pairs={{8,0},{16,8},{24,16},{32,24},{40,32},{48,40},{56,48},{64,56},{72,6... | collective-permute-start | bytes 688136 | tf_op jit(solution)/shard_map/ppermute | solution.py:383
  40.0 3.6 %shard_map.79 = (bf16[25,128,896]{2,1,0:T(8,128)(2,1)S(1)}, bf16[25,48,336]{2,1,0:T(8,128)(2,1)S(1)}, bf16[800,200]{1,0:T(8,128)(2,1)S(1)}, f32[200,128]{1,0:T(8,128)S(1)}) custom-call(bf16[3,7,7,200]{3,2,1,0:T(8,128)(2,1)S(1)} %bitcast.7, bf16[3,200,800]{2,1,0:T(8,128)(2,1)S(1)} %copy-done.3, bf16[3,200]{1,0:T(4,128)(2,1)S(1)} %copy-done.7), custom_call_target="tpu_custom_call" | custom-call | flops 2147483648 | bytes 9000000 | tf_op jit(solution)/shard_map/pallas_call | solution.py:96
  43.7 1.7 %shard_map.78 = (bf16[640,128]{1,0:T(8,128)(2,1)S(1)}, bf16[640,128]{1,0:T(8,128)(2,1)}) custom-call(s32[2048]{0:T(1024)S(1)} %copy-done.1, bf16[896,128]{1,0:T(8,128)(2,1)S(1)} %collective-permute-done.52.west_ref, bf16[896,128]{1,0:T(8,128)(2,1)S(1)} %collective-permute-done.53.east_ref, bf16[896,128]{1,0:T(8,128)(2,1)S(1)} %get-tuple-element.1064.send_ref, ...), custom_call_target="tpu_custom_call" | custom-call | tf_op jit(solution)/shard_map/pallas_call | solution.py:215
  45.4 6.0 %collective-permute-start.54 = (bf16[640,128]{1,0:T(8,128)(2,1)S(1)}, bf16[640,128]{1,0:T(8,128)(2,1)S(1)}, u32[]{:S(2)}, u32[]{:S(2)}) collective-permute-start(bf16[640,128]{1,0:T(8,128)(2,1)S(1)} %get-tuple-element.1070), channel_id=1, source_target_pairs={{0,1},{1,0},{2,3},{3,2},{4,5},{5,4},{6,7},{7,6},{8,9},{9,8},{10,11... | collective-permute-start | bytes 491528 | tf_op jit(solution)/shard_map/ppermute | solution.py:386
  51.4 1.9 %collective-permute-start.55 = (bf16[640,128]{1,0:T(8,128)(2,1)}, bf16[640,128]{1,0:T(8,128)(2,1)S(1)}, u32[]{:S(2)}, u32[]{:S(2)}) collective-permute-start(bf16[640,128]{1,0:T(8,128)(2,1)} %get-tuple-element.1071), channel_id=1, source_target_pairs={{1,2},{2,1},{3,4},{4,3},{5,6},{6,5},{9,10},{10,9},{11,12},{12,11},... | collective-permute-start | bytes 491528 | tf_op jit(solution)/shard_map/ppermute | solution.py:387
  53.3 4.1 %shard_map.80.refs_1_ = f32[16,25,8,128]{3,2,1,0:T(8,128)} custom-call(bf16[200,16,128]{2,1,0:T(8,128)(2,1)S(1)} %get-tuple-element.1063.x_ref.refs_0_, bf16[25,128,896]{2,1,0:T(8,128)(2,1)S(1)} %get-tuple-element.1067.band_ref, bf16[896,128]{1,0:T(8,128)(2,1)S(1)} %collective-permute-done.52.west_ref, bf16[896,128]{1,0:T(8,128)(2,1)S(1)} %collective-permute-done.53.east_ref), custom_call_target="tpu_custom_call" | custom-call | flops 3355443200 | bytes 9000000 | tf_op jit(solution)/shard_map/pallas_call | solution.py:262
  57.4 1.3 %conditional.4 = (bf16[640,128]{1,0:T(8,128)(2,1)}, f32[16,128]{1,0:T(8,128)S(1)}) conditional(s32[]{:T(128)} %clamp.2, (bf16[640,128]{1,0:T(8,128)(2,1)}, s32[16,128]{1,0:T(8,128)S(1)}, bf16[200,16,128]{2,1,0:T(8,128)(2,1)S(1)}, f32[16,25,8,128]{3,2,1,0:T(8,128)}, bf16[25,48,336]{2,1,0:T(8,128)(2,1)S(1)}, ...), branch_computations={%region_16.17_spmd, %region_17.18_spmd, %region_18.19_spmd, %regio... | conditional | bytes 655416 | solution.py:390
  57.4 1.3 %collective-permute-start.31 = (bf16[640,128]{1,0:T(8,128)(2,1)}, bf16[640,128]{1,0:T(8,128)(2,1)}, u32[]{:S(2)}, u32[]{:S(2)}) collective-permute-start(bf16[640,128]{1,0:T(8,128)(2,1)} %get-tuple-element.894), channel_id=1, source_target_pairs={{7,127},{15,119},{23,111},{31,103},{39,95},{47,87},{55,79},{63,71}... | collective-permute-start | bytes 491528 | tf_op jit(solution)/shard_map/cond/branch_15_fun/ppermute | solution.py:372
  58.7 3.4 %collective-permute-done.55.refs_4_ = bf16[640,128]{1,0:T(8,128)(2,1)S(1)} collective-permute-done((bf16[640,128]{1,0:T(8,128)(2,1)}, bf16[640,128]{1,0:T(8,128)(2,1)S(1)}, u32[]{:S(2)}, u32[]{:S(2)}) %collective-permute-start.55) | collective-permute-done | bytes 163872 | tf_op jit(solution)/shard_map/ppermute | solution.py:387
  62.1 6.4 %shard_map.81 = (bf16[200,16,128]{2,1,0:T(8,128)(2,1)S(1)}, bf16[896,128]{1,0:T(8,128)(2,1)S(1)}, bf16[608,128]{1,0:T(8,128)(2,1)S(1)}) custom-call(bf16[200,16,128]{2,1,0:T(8,128)(2,1)} %copy-done.11, f32[16,25,8,128]{3,2,1,0:T(8,128)} %shard_map.80.refs_1_, bf16[25,48,336]{2,1,0:T(8,128)(2,1)} %copy-done.8, ...), custom_call_target="tpu_custom_call" | custom-call | tf_op jit(solution)/shard_map/pallas_call | solution.py:344
  68.5 3.8 %collective-permute-start.57 = (bf16[896,128]{1,0:T(8,128)(2,1)S(1)}, bf16[896,128]{1,0:T(8,128)(2,1)S(1)}, u32[]{:S(2)}, u32[]{:S(2)}) collective-permute-start(bf16[896,128]{1,0:T(8,128)(2,1)S(1)} %get-tuple-element.1077.send_ref), channel_id=1, source_target_pairs={{8,0},{16,8},{24,16},{32,24},{40,32},{48,40},{56,48},{64,56},{72,6... | collective-permute-start | bytes 688136 | tf_op jit(solution)/shard_map/ppermute | solution.py:383
  72.3 3.6 %shard_map.83 = (bf16[25,128,896]{2,1,0:T(8,128)(2,1)S(1)}, bf16[25,48,336]{2,1,0:T(8,128)(2,1)S(1)}, bf16[800,200]{1,0:T(8,128)(2,1)S(1)}, f32[200,128]{1,0:T(8,128)S(1)}) custom-call(bf16[3,7,7,200]{3,2,1,0:T(8,128)(2,1)S(1)} %bitcast.8, bf16[3,200,800]{2,1,0:T(8,128)(2,1)S(1)} %copy-done.3, bf16[3,200]{1,0:T(4,128)(2,1)S(1)} %copy-done.7), custom_call_target="tpu_custom_call" | custom-call | flops 2147483648 | bytes 9000000 | tf_op jit(solution)/shard_map/pallas_call | solution.py:96
  76.0 1.5 %shard_map.82 = (bf16[640,128]{1,0:T(8,128)(2,1)S(1)}, bf16[640,128]{1,0:T(8,128)(2,1)}) custom-call(s32[2048]{0:T(1024)S(1)} %copy-done.1, bf16[896,128]{1,0:T(8,128)(2,1)S(1)} %collective-permute-done.56.west_ref, bf16[896,128]{1,0:T(8,128)(2,1)S(1)} %collective-permute-done.57.east_ref, bf16[896,128]{1,0:T(8,128)(2,1)S(1)} %get-tuple-element.1077.send_ref, ...), custom_call_target="tpu_custom_call" | custom-call | tf_op jit(solution)/shard_map/pallas_call | solution.py:215
  77.5 4.1 %collective-permute-start.58 = (bf16[640,128]{1,0:T(8,128)(2,1)S(1)}, bf16[640,128]{1,0:T(8,128)(2,1)S(1)}, u32[]{:S(2)}, u32[]{:S(2)}) collective-permute-start(bf16[640,128]{1,0:T(8,128)(2,1)S(1)} %get-tuple-element.1083), channel_id=1, source_target_pairs={{0,1},{1,0},{2,3},{3,2},{4,5},{5,4},{6,7},{7,6},{8,9},{9,8},{10,11... | collective-permute-start | bytes 491528 | tf_op jit(solution)/shard_map/ppermute | solution.py:386
  81.6 1.9 %collective-permute-start.59 = (bf16[640,128]{1,0:T(8,128)(2,1)}, bf16[640,128]{1,0:T(8,128)(2,1)S(1)}, u32[]{:S(2)}, u32[]{:S(2)}) collective-permute-start(bf16[640,128]{1,0:T(8,128)(2,1)} %get-tuple-element.1084), channel_id=1, source_target_pairs={{1,2},{2,1},{3,4},{4,3},{5,6},{6,5},{9,10},{10,9},{11,12},{12,11},... | collective-permute-start | bytes 491528 | tf_op jit(solution)/shard_map/ppermute | solution.py:387
  83.5 2.9 %shard_map.84.refs_1_ = f32[16,25,8,128]{3,2,1,0:T(8,128)S(1)} custom-call(bf16[200,16,128]{2,1,0:T(8,128)(2,1)S(1)} %get-tuple-element.1076.x_ref.refs_0_, bf16[25,128,896]{2,1,0:T(8,128)(2,1)S(1)} %get-tuple-element.1080.band_ref, bf16[896,128]{1,0:T(8,128)(2,1)S(1)} %collective-permute-done.56.west_ref, bf16[896,128]{1,0:T(8,128)(2,1)S(1)} %collective-permute-done.57.east_ref), custom_call_target="tpu_custom_call" | custom-call | flops 3355443200 | bytes 9000000 | tf_op jit(solution)/shard_map/pallas_call | solution.py:262
  86.5 1.6 %conditional.5 = (bf16[640,128]{1,0:T(8,128)(2,1)}, f32[16,128]{1,0:T(8,128)S(1)}) conditional(s32[]{:T(128)} %clamp.2, (bf16[640,128]{1,0:T(8,128)(2,1)}, s32[16,128]{1,0:T(8,128)S(1)}, bf16[200,16,128]{2,1,0:T(8,128)(2,1)S(1)}, f32[16,25,8,128]{3,2,1,0:T(8,128)S(1)}, bf16[25,48,336]{2,1,0:T(8,128)(2,1)S(1)}, ...), branch_computations={%region_32.33_spmd, %region_33.34_spmd, %region_34.35_spmd, %regio... | conditional | bytes 655416 | solution.py:390
  86.7 1.3 %collective-permute-start.47 = (bf16[640,128]{1,0:T(8,128)(2,1)}, bf16[640,128]{1,0:T(8,128)(2,1)}, u32[]{:S(2)}, u32[]{:S(2)}) collective-permute-start(bf16[640,128]{1,0:T(8,128)(2,1)} %get-tuple-element.1006), channel_id=1, source_target_pairs={{7,127},{15,119},{23,111},{31,103},{39,95},{47,87},{55,79},{63,71}... | collective-permute-start | bytes 491528 | tf_op jit(solution)/shard_map/cond/branch_15_fun/ppermute | solution.py:372
  88.1 4.4 %collective-permute-done.59.refs_4_ = bf16[640,128]{1,0:T(8,128)(2,1)S(1)} collective-permute-done((bf16[640,128]{1,0:T(8,128)(2,1)}, bf16[640,128]{1,0:T(8,128)(2,1)S(1)}, u32[]{:S(2)}, u32[]{:S(2)}) %collective-permute-start.59) | collective-permute-done | bytes 163872 | tf_op jit(solution)/shard_map/ppermute | solution.py:387
  92.5 6.4 %shard_map.85 = bf16[200,16,128]{2,1,0:T(8,128)(2,1)} custom-call(bf16[200,16,128]{2,1,0:T(8,128)(2,1)} %copy-done.12, f32[16,25,8,128]{3,2,1,0:T(8,128)S(1)} %shard_map.84.refs_1_, bf16[25,48,336]{2,1,0:T(8,128)(2,1)} %copy-done.9, bf16[640,128]{1,0:T(8,128)(2,1)S(1)} %collective-permute-done.58.refs_3_, ...), custom_call_target="tpu_custom_call" | custom-call | tf_op jit(solution)/shard_map/pallas_call | solution.py:344
  (52 shorter events, 3.3 us)
Async XLA Ops:
  1.7 12.3 %collective-permute-start.48 = (bf16[896,128]{1,0:T(8,128)(2,1)S(1)}, bf16[896,128]{1,0:T(8,128)(2,1)S(1)}, u32[]{:S(2)}, u32[]{:S(2)}) collective-permute-start(bf16[896,128]{1,0:T(8,128)(2,1)S(1)} %get-tuple-element.1051.send_ref), channel_id=1, source_target_pairs={{0,8},{8,16},{16,24},{24,32},{32,40},{40,48},{48,56},{56,64},{64,7... | collective-permute-start | bytes 688136 | tf_op jit(solution)/shard_map/ppermute | solution.py:382
  1.8 12.2 %collective-permute-start.49 = (bf16[896,128]{1,0:T(8,128)(2,1)S(1)}, bf16[896,128]{1,0:T(8,128)(2,1)S(1)}, u32[]{:S(2)}, u32[]{:S(2)}) collective-permute-start(bf16[896,128]{1,0:T(8,128)(2,1)S(1)} %get-tuple-element.1051.send_ref), channel_id=1, source_target_pairs={{8,0},{16,8},{24,16},{32,24},{40,32},{48,40},{56,48},{64,56},{72,6... | collective-permute-start | bytes 688136 | tf_op jit(solution)/shard_map/ppermute | solution.py:383
  7.6 1.2 %copy-start.2 = (bf16[3,200,800]{2,1,0:T(8,128)(2,1)S(1)}, bf16[3,200,800]{2,1,0:T(8,128)(2,1)}, u32[]{:S(2)}) copy-start(bf16[3,200,800]{2,1,0:T(8,128)(2,1)} %refs_1_.5) | copy-start | bytes 2880004
  8.8 0.9 copy-start.4
  9.7 0.7 copy-start.6
  10.4 3.6 %copy-start.1 = (s32[2048]{0:T(1024)S(1)}, s32[2048]{0:T(1024)}, u32[]{:S(2)}) copy-start(s32[2048]{0:T(1024)} %fold_ref.5) | copy-start | bytes 24580
  10.4 11.6 %copy-start.10 = (bf16[200,16,128]{2,1,0:T(8,128)(2,1)S(1)}, bf16[200,16,128]{2,1,0:T(8,128)(2,1)}, u32[]{:S(2)}) copy-start(bf16[200,16,128]{2,1,0:T(8,128)(2,1)} %refs_0_.1) | copy-start | bytes 2457604
  14.0 12.1 %copy-start.13 = (bf16[800,200]{1,0:T(8,128)(2,1)}, bf16[800,200]{1,0:T(8,128)(2,1)S(1)}, u32[]{:S(2)}) copy-start(bf16[800,200]{1,0:T(8,128)(2,1)S(1)} %get-tuple-element.1059.refs_6_) | copy-start | bytes 960004
  14.0 12.1 %copy-start.15 = (f32[200,128]{1,0:T(8,128)}, f32[200,128]{1,0:T(8,128)S(1)}, u32[]{:S(2)}) copy-start(f32[200,128]{1,0:T(8,128)S(1)} %get-tuple-element.1060.refs_8_) | copy-start | bytes 307204
  15.5 12.2 %collective-permute-start.50 = (bf16[640,128]{1,0:T(8,128)(2,1)S(1)}, bf16[640,128]{1,0:T(8,128)(2,1)S(1)}, u32[]{:S(2)}, u32[]{:S(2)}) collective-permute-start(bf16[640,128]{1,0:T(8,128)(2,1)S(1)} %get-tuple-element.1057), channel_id=1, source_target_pairs={{0,1},{1,0},{2,3},{3,2},{4,5},{5,4},{6,7},{7,6},{8,9},{9,8},{10,11... | collective-permute-start | bytes 491528 | tf_op jit(solution)/shard_map/ppermute | solution.py:386
  20.1 9.8 %collective-permute-start.51 = (bf16[640,128]{1,0:T(8,128)(2,1)}, bf16[640,128]{1,0:T(8,128)(2,1)S(1)}, u32[]{:S(2)}, u32[]{:S(2)}) collective-permute-start(bf16[640,128]{1,0:T(8,128)(2,1)} %get-tuple-element.1058), channel_id=1, source_target_pairs={{1,2},{2,1},{3,4},{4,3},{5,6},{6,5},{9,10},{10,9},{11,12},{12,11},... | collective-permute-start | bytes 491528 | tf_op jit(solution)/shard_map/ppermute | solution.py:387
  22.0 4.1 %copy-start.16 = (s32[16,128]{1,0:T(8,128)S(1)}, s32[16,128]{1,0:T(8,128)}, u32[]{:S(2)}) copy-start(s32[16,128]{1,0:T(8,128)} %param.56) | copy-start | bytes 24580
  26.1 3.8 %copy-start = (bf16[3,800,200]{1,2,0:T(8,128)(2,1)S(1)}, bf16[3,800,200]{1,2,0:T(8,128)(2,1)}, u32[]{:S(2)}) copy-start(bf16[3,800,200]{1,2,0:T(8,128)(2,1)} %param.61) | copy-start | bytes 2880004
  26.2 1.5 %collective-permute-start.15 = (bf16[640,128]{1,0:T(8,128)(2,1)}, bf16[640,128]{1,0:T(8,128)(2,1)}, u32[]{:S(2)}, u32[]{:S(2)}) collective-permute-start(bf16[640,128]{1,0:T(8,128)(2,1)} %get-tuple-element.782), channel_id=1, source_target_pairs={{7,127},{15,119},{23,111},{31,103},{39,95},{47,87},{55,79},{63,71}... | collective-permute-start | bytes 491528 | tf_op jit(solution)/shard_map/cond/branch_15_fun/ppermute | solution.py:372
  29.9 10.2 %copy-start.3 = (bf16[3,200,800]{2,1,0:T(8,128)(2,1)S(1)}, bf16[3,200,800]{2,1,0:T(8,128)(2,1)}, u32[]{:S(2)}) copy-start(bf16[3,200,800]{2,1,0:T(8,128)(2,1)} %refs_1_.5) | copy-start | bytes 2880004
  29.9 10.2 %copy-start.5 = (bf16[3,200,7,7]{1,3,2,0:T(8,128)(2,1)S(1)}, bf16[3,200,7,7]{1,3,2,0:T(8,128)(2,1)}, u32[]{:S(2)}) copy-start(bf16[3,200,7,7]{1,3,2,0:T(8,128)(2,1)} %param.58) | copy-start | bytes 176404
  29.9 10.2 %copy-start.7 = (bf16[3,200]{1,0:T(4,128)(2,1)S(1)}, bf16[3,200]{1,0:T(4,128)(2,1)}, u32[]{:S(2)}) copy-start(bf16[3,200]{1,0:T(4,128)(2,1)} %refs_2_.5) | copy-start | bytes 3604
  36.1 21.3 %copy-start.11 = (bf16[200,16,128]{2,1,0:T(8,128)(2,1)}, bf16[200,16,128]{2,1,0:T(8,128)(2,1)S(1)}, u32[]{:S(2)}) copy-start(bf16[200,16,128]{2,1,0:T(8,128)(2,1)S(1)} %get-tuple-element.1063.x_ref.refs_0_) | copy-start | bytes 2457604
  36.1 7.6 %collective-permute-start.52 = (bf16[896,128]{1,0:T(8,128)(2,1)S(1)}, bf16[896,128]{1,0:T(8,128)(2,1)S(1)}, u32[]{:S(2)}, u32[]{:S(2)}) collective-permute-start(bf16[896,128]{1,0:T(8,128)(2,1)S(1)} %get-tuple-element.1064.send_ref), channel_id=1, source_target_pairs={{0,8},{8,16},{16,24},{24,32},{32,40},{40,48},{48,56},{56,64},{64,7... | collective-permute-start | bytes 688136 | tf_op jit(solution)/shard_map/ppermute | solution.py:382
  36.2 7.5 %collective-permute-start.53 = (bf16[896,128]{1,0:T(8,128)(2,1)S(1)}, bf16[896,128]{1,0:T(8,128)(2,1)S(1)}, u32[]{:S(2)}, u32[]{:S(2)}) collective-permute-start(bf16[896,128]{1,0:T(8,128)(2,1)S(1)} %get-tuple-element.1064.send_ref), channel_id=1, source_target_pairs={{8,0},{16,8},{24,16},{32,24},{40,32},{48,40},{56,48},{64,56},{72,6... | collective-permute-start | bytes 688136 | tf_op jit(solution)/shard_map/ppermute | solution.py:383
  43.6 13.7 %copy-start.8 = (bf16[25,48,336]{2,1,0:T(8,128)(2,1)}, bf16[25,48,336]{2,1,0:T(8,128)(2,1)S(1)}, u32[]{:S(2)}) copy-start(bf16[25,48,336]{2,1,0:T(8,128)(2,1)S(1)} %get-tuple-element.1069.refs_2_) | copy-start | bytes 2419204
  45.4 13.3 %collective-permute-start.54 = (bf16[640,128]{1,0:T(8,128)(2,1)S(1)}, bf16[640,128]{1,0:T(8,128)(2,1)S(1)}, u32[]{:S(2)}, u32[]{:S(2)}) collective-permute-start(bf16[640,128]{1,0:T(8,128)(2,1)S(1)} %get-tuple-element.1070), channel_id=1, source_target_pairs={{0,1},{1,0},{2,3},{3,2},{4,5},{5,4},{6,7},{7,6},{8,9},{9,8},{10,11... | collective-permute-start | bytes 491528 | tf_op jit(solution)/shard_map/ppermute | solution.py:386
  51.4 10.7 %collective-permute-start.55 = (bf16[640,128]{1,0:T(8,128)(2,1)}, bf16[640,128]{1,0:T(8,128)(2,1)S(1)}, u32[]{:S(2)}, u32[]{:S(2)}) collective-permute-start(bf16[640,128]{1,0:T(8,128)(2,1)} %get-tuple-element.1071), channel_id=1, source_target_pairs={{1,2},{2,1},{3,4},{4,3},{5,6},{6,5},{9,10},{10,9},{11,12},{12,11},... | collective-permute-start | bytes 491528 | tf_op jit(solution)/shard_map/ppermute | solution.py:387
  57.4 1.3 %collective-permute-start.31 = (bf16[640,128]{1,0:T(8,128)(2,1)}, bf16[640,128]{1,0:T(8,128)(2,1)}, u32[]{:S(2)}, u32[]{:S(2)}) collective-permute-start(bf16[640,128]{1,0:T(8,128)(2,1)} %get-tuple-element.894), channel_id=1, source_target_pairs={{7,127},{15,119},{23,111},{31,103},{39,95},{47,87},{55,79},{63,71}... | collective-permute-start | bytes 491528 | tf_op jit(solution)/shard_map/cond/branch_15_fun/ppermute | solution.py:372
  68.4 18.0 %copy-start.12 = (bf16[200,16,128]{2,1,0:T(8,128)(2,1)}, bf16[200,16,128]{2,1,0:T(8,128)(2,1)S(1)}, u32[]{:S(2)}) copy-start(bf16[200,16,128]{2,1,0:T(8,128)(2,1)S(1)} %get-tuple-element.1076.x_ref.refs_0_) | copy-start | bytes 2457604
  68.4 7.6 %collective-permute-start.56 = (bf16[896,128]{1,0:T(8,128)(2,1)S(1)}, bf16[896,128]{1,0:T(8,128)(2,1)S(1)}, u32[]{:S(2)}, u32[]{:S(2)}) collective-permute-start(bf16[896,128]{1,0:T(8,128)(2,1)S(1)} %get-tuple-element.1077.send_ref), channel_id=1, source_target_pairs={{0,8},{8,16},{16,24},{24,32},{32,40},{40,48},{48,56},{56,64},{64,7... | collective-permute-start | bytes 688136 | tf_op jit(solution)/shard_map/ppermute | solution.py:382
  68.5 7.5 %collective-permute-start.57 = (bf16[896,128]{1,0:T(8,128)(2,1)S(1)}, bf16[896,128]{1,0:T(8,128)(2,1)S(1)}, u32[]{:S(2)}, u32[]{:S(2)}) collective-permute-start(bf16[896,128]{1,0:T(8,128)(2,1)S(1)} %get-tuple-element.1077.send_ref), channel_id=1, source_target_pairs={{8,0},{16,8},{24,16},{32,24},{40,32},{48,40},{56,48},{64,56},{72,6... | collective-permute-start | bytes 688136 | tf_op jit(solution)/shard_map/ppermute | solution.py:383
  75.9 10.5 %copy-start.9 = (bf16[25,48,336]{2,1,0:T(8,128)(2,1)}, bf16[25,48,336]{2,1,0:T(8,128)(2,1)S(1)}, u32[]{:S(2)}) copy-start(bf16[25,48,336]{2,1,0:T(8,128)(2,1)S(1)} %get-tuple-element.1082.refs_2_) | copy-start | bytes 2419204
  75.9 10.5 %copy-start.14 = (bf16[800,200]{1,0:T(8,128)(2,1)}, bf16[800,200]{1,0:T(8,128)(2,1)S(1)}, u32[]{:S(2)}) copy-start(bf16[800,200]{1,0:T(8,128)(2,1)S(1)} %get-tuple-element.1085.refs_6_) | copy-start | bytes 960004
  77.5 10.6 %collective-permute-start.58 = (bf16[640,128]{1,0:T(8,128)(2,1)S(1)}, bf16[640,128]{1,0:T(8,128)(2,1)S(1)}, u32[]{:S(2)}, u32[]{:S(2)}) collective-permute-start(bf16[640,128]{1,0:T(8,128)(2,1)S(1)} %get-tuple-element.1083), channel_id=1, source_target_pairs={{0,1},{1,0},{2,3},{3,2},{4,5},{5,4},{6,7},{7,6},{8,9},{9,8},{10,11... | collective-permute-start | bytes 491528 | tf_op jit(solution)/shard_map/ppermute | solution.py:386
  81.6 10.9 %collective-permute-start.59 = (bf16[640,128]{1,0:T(8,128)(2,1)}, bf16[640,128]{1,0:T(8,128)(2,1)S(1)}, u32[]{:S(2)}, u32[]{:S(2)}) collective-permute-start(bf16[640,128]{1,0:T(8,128)(2,1)} %get-tuple-element.1084), channel_id=1, source_target_pairs={{1,2},{2,1},{3,4},{4,3},{5,6},{6,5},{9,10},{10,9},{11,12},{12,11},... | collective-permute-start | bytes 491528 | tf_op jit(solution)/shard_map/ppermute | solution.py:387
  86.7 1.3 %collective-permute-start.47 = (bf16[640,128]{1,0:T(8,128)(2,1)}, bf16[640,128]{1,0:T(8,128)(2,1)}, u32[]{:S(2)}, u32[]{:S(2)}) collective-permute-start(bf16[640,128]{1,0:T(8,128)(2,1)} %get-tuple-element.1006), channel_id=1, source_target_pairs={{7,127},{15,119},{23,111},{31,103},{39,95},{47,87},{55,79},{63,71}... | collective-permute-start | bytes 491528 | tf_op jit(solution)/shard_map/cond/branch_15_fun/ppermute | solution.py:372
